TPU v7x, 32 devices: a whole 2x2x4 slice. The times are simulated.
32 devices in a mesh: grp: 2 (over x), tile: 16 (over z, y, core).
Axes of the slice: x: 2, y: 2, z: 4, core: 2. Of those that a mesh axis runs over, the one named last changes fastest.
Arguments:
- mask_params: float32 [64, 64, 128], P(('grp', 'tile')), parts along dimension 0, may hold values from -3 to 3
- target: float32 [64, 64, 128], P(('grp', 'tile')), parts along dimension 0, may hold values from 0 to 1
- weight: float32 [64, 64, 128], P(('grp', 'tile')), parts along dimension 0, may hold values from 0.3 to 3
- kernels: float32 [24, 2, 65, 65], replicated, may hold values from -0.25515518 to 0.25515518
- kernel_weight: float32 [24], replicated, may hold values from 0.05 to 1
- tile_ids: int32 [64], P(('grp', 'tile')), parts along dimension 0, may hold values from -1 to 134, as said below
- tile_links: int32 [64, 2], P(('grp', 'tile')), parts along dimension 0, may hold values from 0 to 1, as said below
Outputs:
- params_out: float32 [64, 64, 128], P(('grp', 'tile')), parts along dimension 0
- resist: float32 [64, 64, 128], P(('grp', 'tile')), parts along dimension 0
There are 2 independent parts, one for each index of `grp`. A program takes and returns all parts, laid end to end along the dimension named above; an argument that names none is the same for every part. Nothing has to cross between parts.
Inputs may be any that keep to these rules, and one draw needn't show every extreme that they name: `tile_ids`: -1 marks an empty slot. Every device holds between 1 and 2 tiles in its first slots and some device holds 2; stripe columns rise strictly in the order of devices and slots, and the last live tile of the stripe holds column 134. `tile_links`: entry 0 is 1 exactly where the stripe column just before the slot's tile holds an active tile (then held by the previous live slot in order), entry 1 likewise for the column just after (the next live slot); both are 0 for empty slots.
All inputs are finite; a program needn't handle non-finite values.
Results may differ from a plain program's by a relative error of at most 0.00011.
Values sent between devices are 32-bit elements; how exact they have to be, the bound alone decides.
A program may use at most 64 MiB of HBM per device.

v0:
```python
import functools
import math

import jax
import jax.numpy as jnp
import ml_dtypes
import numpy as np
from jax import lax
from jax.experimental import pallas as pl
from jax.experimental.pallas import tpu as pltpu
from jax.sharding import PartitionSpec as P

ITERS = 2
RESIST_SLOPE = 4.0
THRESHOLD = 0.9
STEP_SCALE = 0.04
F32 = jnp.float32
BF16 = jnp.bfloat16


def round_up(size, step):
    return (size + step - 1) // step * step


def phases(length, period, bands):
    f = np.arange(bands, dtype=np.int64) - (bands - 1) // 2
    turns = (np.arange(length, dtype=np.int64)[:, None] * f[None, :]) % period
    angles = turns.astype(np.float64) * (2.0 * math.pi / period)
    return np.cos(angles), np.sin(angles)


def padded(table, rows, cols):
    return np.pad(table, ((0, rows - table.shape[0]), (0, cols - table.shape[1])))


def halves(table):
    table = table.astype(np.float32)
    hi = table.astype(ml_dtypes.bfloat16)
    lo = (table - hi.astype(np.float32)).astype(ml_dtypes.bfloat16)
    return hi, lo


def left_table(table):
    hi, lo = halves(table)
    return np.concatenate([hi, hi, lo], axis=1)


def right_table(table):
    hi, lo = halves(table)
    return np.concatenate([hi, lo, hi], axis=0)


def make_tables(rows, cols, bands):
    fp, fl = round_up(bands, 16), round_up(bands, 128)
    row_cos, row_sin = phases(rows, 2 * rows, bands)
    dom_cos, dom_sin = phases(3 * cols, 3 * cols, bands)
    own = slice(cols, 2 * cols)
    to_rows = np.concatenate([padded(row_cos, rows, fp), padded(row_sin, rows, fp)], axis=1)
    to_freqs = np.concatenate(
        [padded(row_cos.T, fp, rows), padded(row_sin.T, fp, rows)], axis=1
    )
    oc, os = padded(dom_cos[own].T, fl, cols), padded(dom_sin[own].T, fl, cols)
    field = np.block([[oc, os], [-os, oc]])
    adjoint = np.block([[oc.T, os.T], [os.T, -oc.T]])
    dc, ds = padded(dom_cos, 3 * cols, fl), padded(dom_sin, 3 * cols, fl)
    spectrum = np.concatenate([dc, -ds], axis=1)
    gradient = np.concatenate([dc.T, ds.T], axis=0)
    return (
        left_table(to_rows),
        left_table(to_freqs),
        right_table(spectrum),
        right_table(field),
        right_table(adjoint),
        right_table(gradient),
    )


def split(x):
    hi = x.astype(BF16)
    lo = (x - hi.astype(F32)).astype(BF16)
    return hi, lo


def dot(a, b):
    return jnp.dot(a, b, preferred_element_type=F32)


def stream(x, table_ref):
    hi, lo = split(x)
    return dot(jnp.concatenate([hi, hi, lo], axis=1), table_ref[...])


def table_dot(table_ref, x):
    hi, lo = split(x)
    return dot(table_ref[...], jnp.concatenate([hi, lo, hi], axis=0))


def kernel(
    axis,
    n,
    chunk,
    params_ref,
    target_ref,
    weight_ref,
    kernels_ref,
    scale_ref,
    ids_ref,
    links_ref,
    rows_ref,
    freqs_ref,
    spectrum_ref,
    field_ref,
    adjoint_ref,
    gradient_ref,
    out_ref,
    resist_ref,
    h_ref,
    e_ref,
    t_ref,
    send_ref,
    recv_ref,
    send_sems,
    recv_sems,
):
    me = lax.axis_index(axis)
    slots, rows, cols = params_ref.shape
    count, _, bands, _ = kernels_ref.shape
    fp, fl = h_ref.shape[1], h_ref.shape[2] // 2
    unit = 1.0 / (rows * cols)
    step_size = STEP_SCALE * math.sqrt(rows * cols)
    has_left, has_right = me > 0, me < n - 1

    barrier = pltpu.get_barrier_semaphore()

    @pl.when(has_left)
    def _():
        pl.semaphore_signal(
            barrier, inc=1, device_id={axis: me - 1}, device_id_type=pl.DeviceIdType.MESH
        )

    @pl.when(has_right)
    def _():
        pl.semaphore_signal(
            barrier, inc=1, device_id={axis: me + 1}, device_id_type=pl.DeviceIdType.MESH
        )

    peers = jnp.where(has_left, 1, 0) + jnp.where(has_right, 1, 0)
    pl.semaphore_wait(barrier, peers)

    @pl.when(jnp.logical_not(has_left))
    def _():
        for e in range(2 * ITERS):
            recv_ref[e, 0] = jnp.zeros((rows, cols), F32)

    @pl.when(jnp.logical_not(has_right))
    def _():
        for e in range(2 * ITERS):
            recv_ref[e, 1] = jnp.zeros((rows, cols), F32)

    def move(e, side):
        return pltpu.make_async_remote_copy(
            src_ref=send_ref.at[e, side],
            dst_ref=recv_ref.at[e, side],
            send_sem=send_sems.at[e, side],
            recv_sem=recv_sems.at[e, side],
            device_id={axis: me + 1 if side == 0 else me - 1},
            device_id_type=pl.DeviceIdType.MESH,
        )

    def start(e):
        @pl.when(has_right)
        def _():
            move(e, 0).start()

        @pl.when(has_left)
        def _():
            move(e, 1).start()

    def arrive(e):
        @pl.when(has_left)
        def _():
            move(e, 0).wait_recv()

        @pl.when(has_right)
        def _():
            move(e, 1).wait_recv()

    live = [ids_ref[s] >= 0 for s in range(slots)]
    left_on = [jnp.where(links_ref[s, 0] == 1, 1.0, 0.0) for s in range(slots)]
    right_on = [jnp.where(links_ref[s, 1] == 1, 1.0, 0.0) for s in range(slots)]

    def last_live(values):
        last = values[0]
        for s in range(1, slots):
            last = jnp.where(live[s], values[s], last)
        return last

    def neighbours(to_right, to_left, e):
        befores, afters = [], []
        for s in range(slots):
            before = recv_ref[e, 0] if s == 0 else to_right[s - 1]
            after = recv_ref[e, 1]
            if s + 1 < slots:
                after = jnp.where(live[s + 1], to_left[s + 1], after)
            befores.append(before * left_on[s])
            afters.append(after * right_on[s])
        return befores, afters

    for it in range(ITERS):
        source = params_ref if it == 0 else out_ref
        transmit = [jnp.tanh(source[s]) for s in range(slots)]
        for s in range(slots):
            t_ref[s] = transmit[s]
        send_ref[2 * it, 0] = last_live(transmit)
        send_ref[2 * it, 1] = transmit[0]
        start(2 * it)

        if it == 0:

            def prepare(k, carry):
                scale = jnp.sqrt(jnp.full((bands, bands), scale_ref[k], F32))
                h_ref[k] = jnp.zeros((fp, 2 * fl), F32)
                h_ref[k, :bands, :bands] = kernels_ref[k, 0] * scale
                h_ref[k, :bands, fl : fl + bands] = kernels_ref[k, 1] * scale
                return carry

            lax.fori_loop(0, count, prepare, 0)

        arrive(2 * it)
        transmit = [t_ref[s] for s in range(slots)]
        befores, afters = neighbours(transmit, transmit, 2 * it)
        domain = jnp.concatenate(
            [
                jnp.concatenate([befores[s], transmit[s], afters[s]], axis=1)
                for s in range(slots)
            ],
            axis=0,
        )
        parts = stream(domain, spectrum_ref)
        spectra = []
        for s in range(slots):
            pr = parts[s * rows : (s + 1) * rows, :fl]
            pi = parts[s * rows : (s + 1) * rows, fl:]
            top = jnp.concatenate([pr, pi], axis=1)
            low = jnp.concatenate([pi, -pr], axis=1)
            spectra.append(table_dot(freqs_ref, jnp.concatenate([top, low], axis=0)) * unit)

        def forward(c, intensities):
            out = []
            for s in range(slots):
                cr, ci = spectra[s][:, :fl], spectra[s][:, fl:]
                mids = []
                for j in range(chunk):
                    k = c * chunk + j
                    hr, hi = h_ref[k, :, :fl], h_ref[k, :, fl:]
                    dr = hr * cr - hi * ci
                    di = hr * ci + hi * cr
                    top = jnp.concatenate([dr, di], axis=1)
                    low = jnp.concatenate([-di, dr], axis=1)
                    mids.append(table_dot(rows_ref, jnp.concatenate([top, low], axis=0)))
                fields = stream(jnp.concatenate(mids, axis=0), field_ref)
                e_ref[s, c] = fields
                total = intensities[s]
                for j in range(chunk):
                    er = fields[j * rows : (j + 1) * rows, :cols]
                    ei = fields[j * rows : (j + 1) * rows, cols:]
                    total = total + er * er + ei * ei
                out.append(total)
            return tuple(out)

        zero = jnp.zeros((rows, cols), F32)
        intensities = lax.fori_loop(0, count // chunk, forward, (zero,) * slots)

        slopes = []
        for s in range(slots):
            now = jax.nn.sigmoid(RESIST_SLOPE * (intensities[s] - THRESHOLD))
            if it == ITERS - 1:
                resist_ref[s] = jnp.where(live[s], now, 0.0)
            slope = 2.0 * weight_ref[s] * (now - target_ref[s]) * RESIST_SLOPE * now * (1.0 - now)
            slopes.append(jnp.concatenate([slope, slope], axis=1))

        def backward(c, sums):
            out = []
            for s in range(slots):
                fields = e_ref[s, c]
                back = jnp.concatenate(
                    [fields[j * rows : (j + 1) * rows] * slopes[s] for j in range(chunk)], axis=0
                )
                columns = stream(back, adjoint_ref)
                sr, si = sums[s]
                for j in range(chunk):
                    k = c * chunk + j
                    gr = columns[j * rows : (j + 1) * rows, :fl]
                    gi = columns[j * rows : (j + 1) * rows, fl:]
                    top = jnp.concatenate([gr, gi], axis=1)
                    low = jnp.concatenate([-gi, gr], axis=1)
                    freq = table_dot(freqs_ref, jnp.concatenate([top, low], axis=0))
                    fr, fi = freq[:, :fl], freq[:, fl:]
                    hr, hi = h_ref[k, :, :fl], h_ref[k, :, fl:]
                    sr = sr + hr * fr - hi * fi
                    si = si + hr * fi + hi * fr
                out.append((sr, si))
            return tuple(out)

        none = jnp.zeros((fp, fl), F32)
        sums = lax.fori_loop(0, count // chunk, backward, ((none, none),) * slots)

        uppers = []
        for s in range(slots):
            sr, si = sums[s]
            top = jnp.concatenate([sr, si], axis=1)
            low = jnp.concatenate([si, -sr], axis=1)
            uppers.append(table_dot(rows_ref, jnp.concatenate([top, low], axis=0)))
        grads = stream(jnp.concatenate(uppers, axis=0), gradient_ref) * (2.0 * unit)
        to_left = [grads[s * rows : (s + 1) * rows, :cols] for s in range(slots)]
        middle = [grads[s * rows : (s + 1) * rows, cols : 2 * cols] for s in range(slots)]
        to_right = [grads[s * rows : (s + 1) * rows, 2 * cols :] for s in range(slots)]
        send_ref[2 * it + 1, 0] = last_live(to_right)
        send_ref[2 * it + 1, 1] = to_left[0]
        start(2 * it + 1)
        arrive(2 * it + 1)
        befores, afters = neighbours(to_right, to_left, 2 * it + 1)
        for s in range(slots):
            gradient = middle[s] + befores[s] + afters[s]
            old = source[s]
            t = t_ref[s]
            new = old - step_size * gradient * (1.0 - t * t)
            out_ref[s] = jnp.where(live[s], new, old)

    for e in range(2 * ITERS):

        @pl.when(has_right)
        def _():
            move(e, 0).wait_send()

        @pl.when(has_left)
        def _():
            move(e, 1).wait_send()


def local(n, mask_params, target, weight, kernels, kernel_weight, tile_ids, tile_links):
    slots, rows, cols = mask_params.shape
    count, _, bands, _ = kernels.shape
    fp, fl = round_up(bands, 16), round_up(bands, 128)
    chunk = next(c for c in (4, 3, 2, 1) if count % c == 0)
    tables = make_tables(rows, cols, bands)
    vmem = pl.BlockSpec(memory_space=pltpu.VMEM)
    smem = pl.BlockSpec(memory_space=pltpu.SMEM)
    shape = jax.ShapeDtypeStruct((slots, rows, cols), F32)
    return pl.pallas_call(
        functools.partial(kernel, "tile", n, chunk),
        out_shape=(shape, shape),
        in_specs=[vmem] * 4 + [smem] * 3 + [vmem] * len(tables),
        out_specs=(vmem, vmem),
        scratch_shapes=[
            pltpu.VMEM((count, fp, 2 * fl), F32),
            pltpu.VMEM((slots, count // chunk, chunk * rows, 2 * cols), F32),
            pltpu.VMEM((slots, rows, cols), F32),
            pltpu.VMEM((2 * ITERS, 2, rows, cols), F32),
            pltpu.VMEM((2 * ITERS, 2, rows, cols), F32),
            pltpu.SemaphoreType.DMA((2 * ITERS, 2)),
            pltpu.SemaphoreType.DMA((2 * ITERS, 2)),
        ],
        compiler_params=pltpu.CompilerParams(
            collective_id=0, has_side_effects=True, vmem_limit_bytes=48 * 1024 * 1024
        ),
    )(
        mask_params,
        target,
        weight,
        kernels,
        kernel_weight,
        tile_ids,
        tile_links,
        *[jnp.asarray(t) for t in tables],
    )


def solution(mesh):
    both = ("grp", "tile")
    return jax.shard_map(
        functools.partial(local, mesh.shape["tile"]),
        mesh=mesh,
        in_specs=(P(both, None, None),) * 3 + (P(), P(), P(both), P(both, None)),
        out_specs=(P(both, None, None),) * 2,
        check_vma=False,
    )
```

profile of v0, /device:TPU:21, one launch (start us, length us, event | category | flops | bytes accessed | tf_op | source)
XLA Modules:
  0.0 42.9 jit_solution(2996635872432664521)
XLA Ops:
  0.6 0.0 copy-start
  0.6 0.0 copy-start.2
  0.7 0.0 copy-start.3
  0.7 0.0 copy-start.1
  0.7 0.0 copy-start.8
  0.7 0.0 copy-start.7
  0.7 0.0 copy-start.9
  0.7 0.0 copy-start.11
  0.7 0.0 copy-start.10
  0.7 0.0 copy-start.6
  0.7 0.0 copy-start.5
  0.8 0.0 copy-start.4
  0.8 1.7 %copy.15.kernels_ref = f32[24,2,65,65]{3,2,1,0:T(8,128)S(1)} copy(f32[24,2,65,65]{3,1,2,0:T(2,128)} %param.16) | data formatting | bytes 1622400 | tf_op args[3]
  2.5 0.0 copy-done
  2.5 0.0 copy-done.2
  2.5 0.0 copy-done.3
  2.5 0.1 copy-done.1
  2.6 0.0 copy-done.8
  2.6 0.0 copy-done.7
  2.6 0.0 copy-done.9
  2.6 0.0 copy-done.11
  2.6 0.0 copy-done.10
  2.6 0.0 copy-done.6
  2.6 0.0 copy-done.5
  2.6 0.0 copy-done.4
  2.7 38.9 %shard_map.140 = (f32[2,64,128]{2,1,0:T(8,128)S(1)}, f32[2,64,128]{2,1,0:T(8,128)S(1)}) custom-call(f32[2,64,128]{2,1,0:T(8,128)S(1)} %copy-done.4, f32[2,64,128]{2,1,0:T(8,128)S(1)} %copy-done.5, f32[2,64,128]{2,1,0:T(8,128)S(1)} %copy-done.6, f32[24,2,65,65]{3,2,1,0:T(8,128)S(1)} %copy.15.kernels_ref, f32[24]{0:T(128)S(1)} %copy-done.10, s32[2]{0:T(128)S(1)} %copy-done.11, ...), custom_call_target="tpu_custom_call" | custom-call | tf_op jit(solution)/shard_map/pallas_call | solution.py:350
  41.6 0.6 %copy.18 = f32[2,64,128]{2,1,0:T(8,128)} copy(f32[2,64,128]{2,1,0:T(8,128)S(1)} %get-tuple-element.4) | data formatting | bytes 131072
  42.2 0.6 %copy.19 = f32[2,64,128]{2,1,0:T(8,128)} copy(f32[2,64,128]{2,1,0:T(8,128)S(1)} %get-tuple-element.5) | data formatting | bytes 131072
Async XLA Ops:
  0.6 1.8 %copy-start = (bf16[768,384]{1,0:T(8,128)(2,1)S(1)}, bf16[768,384]{1,0:T(8,128)(2,1)}, u32[]{:S(2)}) copy-start(bf16[768,384]{1,0:T(8,128)(2,1)} %constant.17.clone.gradient_ref) | copy-start | bytes 1769476
  0.6 1.8 %copy-start.2 = (bf16[768,256]{1,0:T(8,128)(2,1)S(1)}, bf16[768,256]{1,0:T(8,128)(2,1)}, u32[]{:S(2)}) copy-start(bf16[768,256]{1,0:T(8,128)(2,1)} %constant.16.clone.adjoint_ref) | copy-start | bytes 1179652
  0.7 1.8 %copy-start.3 = (bf16[768,256]{1,0:T(8,128)(2,1)S(1)}, bf16[768,256]{1,0:T(8,128)(2,1)}, u32[]{:S(2)}) copy-start(bf16[768,256]{1,0:T(8,128)(2,1)} %constant.15.clone.field_ref) | copy-start | bytes 1179652
  0.7 1.9 %copy-start.1 = (bf16[1152,256]{1,0:T(8,128)(2,1)S(1)}, bf16[1152,256]{1,0:T(8,128)(2,1)}, u32[]{:S(2)}) copy-start(bf16[1152,256]{1,0:T(8,128)(2,1)} %constant.14.clone.spectrum_ref) | copy-start | bytes 1769476
  0.7 1.9 %copy-start.8 = (bf16[80,384]{1,0:T(8,128)(2,1)S(1)}, bf16[80,384]{1,0:T(8,128)(2,1)}, u32[]{:S(2)}) copy-start(bf16[80,384]{1,0:T(8,128)(2,1)} %constant.13.clone.freqs_ref) | copy-start | bytes 184324
  0.7 1.9 %copy-start.7 = (bf16[64,480]{1,0:T(8,128)(2,1)S(1)}, bf16[64,480]{1,0:T(8,128)(2,1)}, u32[]{:S(2)}) copy-start(bf16[64,480]{1,0:T(8,128)(2,1)} %constant.12.clone.rows_ref) | copy-start | bytes 184324
  0.7 1.9 %copy-start.9 = (s32[2,2]{1,0:T(2,128)S(1)}, s32[2,2]{1,0:T(2,128)}, u32[]{:S(2)}) copy-start(s32[2,2]{1,0:T(2,128)} %links_ref.1) | copy-start | bytes 52
  0.7 1.9 %copy-start.11 = (s32[2]{0:T(128)S(1)}, s32[2]{0:T(128)}, u32[]{:S(2)}) copy-start(s32[2]{0:T(128)} %ids_ref.1) | copy-start | bytes 28
  0.7 1.9 %copy-start.10 = (f32[24]{0:T(128)S(1)}, f32[24]{0:T(128)}, u32[]{:S(2)}) copy-start(f32[24]{0:T(128)} %scale_ref.1) | copy-start | bytes 292
  0.7 1.9 %copy-start.6 = (f32[2,64,128]{2,1,0:T(8,128)S(1)}, f32[2,64,128]{2,1,0:T(8,128)}, u32[]{:S(2)}) copy-start(f32[2,64,128]{2,1,0:T(8,128)} %weight_ref.1) | copy-start | bytes 196612
  0.7 1.9 %copy-start.5 = (f32[2,64,128]{2,1,0:T(8,128)S(1)}, f32[2,64,128]{2,1,0:T(8,128)}, u32[]{:S(2)}) copy-start(f32[2,64,128]{2,1,0:T(8,128)} %target_ref.1) | copy-start | bytes 196612
  0.8 1.9 %copy-start.4 = (f32[2,64,128]{2,1,0:T(8,128)S(1)}, f32[2,64,128]{2,1,0:T(8,128)}, u32[]{:S(2)}) copy-start(f32[2,64,128]{2,1,0:T(8,128)} %params_ref.1) | copy-start | bytes 196612
where the time goes:
time: 43 us; the launch traced here: 42.9 us
  Pallas kernels  38.9 us (90%)
  local copies, waits for them, and re-layouts  3.15 us (7%)
  between operations  0.79 us (2%)
    pallas_call x1, Pallas kernels, local(): pl.pallas_call(functools.partial(kernel, 'tile', n, chunk), out_shape=(sh...  38.9 us
    unnamed x27, local copies, waits for them, and re-layouts  3.15 us

commit v1 on v0

--- a/solution.py
+++ b/solution.py
@@ -51,14 +51,14 @@
 
 
 def make_tables(rows, cols, bands):
-    fp, fl = round_up(bands, 16), round_up(bands, 128)
+    mid = (bands - 1) // 2
+    hp, fl = round_up(mid + 1, 8), round_up(bands, 128)
     row_cos, row_sin = phases(rows, 2 * rows, bands)
     dom_cos, dom_sin = phases(3 * cols, 3 * cols, bands)
     own = slice(cols, 2 * cols)
-    to_rows = np.concatenate([padded(row_cos, rows, fp), padded(row_sin, rows, fp)], axis=1)
-    to_freqs = np.concatenate(
-        [padded(row_cos.T, fp, rows), padded(row_sin.T, fp, rows)], axis=1
-    )
+    sides = np.r_[0:cols, 2 * cols : 3 * cols]
+    up_cos, up_sin = padded(row_cos[:, mid:], rows, hp), padded(row_sin[:, mid:], rows, hp)
+    to_rows = np.concatenate([up_cos, up_sin], axis=1)
     oc, os = padded(dom_cos[own].T, fl, cols), padded(dom_sin[own].T, fl, cols)
     field = np.block([[oc, os], [-os, oc]])
     adjoint = np.block([[oc.T, os.T], [os.T, -oc.T]])
@@ -67,12 +67,42 @@
     gradient = np.concatenate([dc.T, ds.T], axis=0)
     return (
         left_table(to_rows),
-        left_table(to_freqs),
-        right_table(spectrum),
+        left_table(to_rows.T),
+        right_table(spectrum[own]),
+        right_table(spectrum[sides]),
         right_table(field),
         right_table(adjoint),
-        right_table(gradient),
+        right_table(gradient[:, own]),
+        right_table(gradient[:, sides]),
+        fold_table(bands),
     )
+
+
+def group_of(bands):
+    return 8 // math.gcd(2 * bands, 8)
+
+
+def window_of(bands, j):
+    size = round_up(2 * bands + 6, 16)
+    begin = min(j * 2 * bands // 8 * 8, group_of(bands) * 2 * bands - size)
+    return begin, size
+
+
+def fold_table(bands):
+    mid = (bands - 1) // 2
+    hp = round_up(mid + 1, 8)
+    tables = []
+    for j in range(group_of(bands)):
+        begin, size = window_of(bands, j)
+        table = np.zeros((4 * hp, size), np.float32)
+        first = j * 2 * bands - begin
+        for part in range(2):
+            for i in range(mid + 1):
+                table[2 * part * hp + i, first + 2 * (mid + i) + part] = 1.0
+                if i > 0:
+                    table[(2 * part + 1) * hp + i, first + 2 * (mid - i) + part] = 1.0
+        tables.append(table)
+    return np.stack(tables).astype(ml_dtypes.bfloat16)
 
 
 def split(x):
@@ -93,6 +123,16 @@
 def table_dot(table_ref, x):
     hi, lo = split(x)
     return dot(table_ref[...], jnp.concatenate([hi, lo, hi], axis=0))
+
+
+def quarters(x, hp, fl):
+    return x[:hp, :fl], x[:hp, fl:], x[hp:, :fl], x[hp:, fl:]
+
+
+def block(a, b, c, d):
+    top = jnp.concatenate([a, b], axis=1)
+    low = jnp.concatenate([c, d], axis=1)
+    return jnp.concatenate([top, low], axis=0)
 
 
 def kernel(
@@ -108,12 +148,16 @@
     links_ref,
     rows_ref,
     freqs_ref,
-    spectrum_ref,
+    own_ref,
+    side_ref,
     field_ref,
     adjoint_ref,
-    gradient_ref,
+    middle_ref,
+    outer_ref,
+    fold_ref,
     out_ref,
     resist_ref,
+    k_ref,
     h_ref,
     e_ref,
     t_ref,
@@ -121,15 +165,19 @@
     recv_ref,
     send_sems,
     recv_sems,
+    load_sem,
 ):
     me = lax.axis_index(axis)
     slots, rows, cols = params_ref.shape
-    count, _, bands, _ = kernels_ref.shape
-    fp, fl = h_ref.shape[1], h_ref.shape[2] // 2
+    count, bands = h_ref.shape[0], k_ref.shape[1]
+    hp, fl = h_ref.shape[1] // 2, h_ref.shape[2] // 2
+    group = group_of(bands)
     unit = 1.0 / (rows * cols)
     step_size = STEP_SCALE * math.sqrt(rows * cols)
     has_left, has_right = me > 0, me < n - 1
 
+    load = pltpu.make_async_copy(kernels_ref, k_ref, load_sem)
+    load.start()
     barrier = pltpu.get_barrier_semaphore()
 
     @pl.when(has_left)
@@ -217,47 +265,54 @@
 
         if it == 0:
 
-            def prepare(k, carry):
-                scale = jnp.sqrt(jnp.full((bands, bands), scale_ref[k], F32))
-                h_ref[k] = jnp.zeros((fp, 2 * fl), F32)
-                h_ref[k, :bands, :bands] = kernels_ref[k, 0] * scale
-                h_ref[k, :bands, fl : fl + bands] = kernels_ref[k, 1] * scale
+            load.wait()
+
+            def prepare(c, carry):
+                span = group * 2 * bands
+                base = pl.multiple_of(c * span, 8)
+                for j in range(group):
+                    begin, size = window_of(bands, j)
+                    k = c * group + j
+                    piece = k_ref[pl.ds(base + begin, size), :]
+                    hi, lo = split(piece)
+                    last = (piece - hi.astype(F32) - lo.astype(F32)).astype(BF16)
+                    fold = fold_ref[j]
+                    folded = dot(fold, hi) + dot(fold, lo) + dot(fold, last)
+                    folded = folded * jnp.sqrt(jnp.full(folded.shape, scale_ref[k], F32))
+                    h_ref[k] = jnp.zeros((2 * hp, 2 * fl), F32)
+                    h_ref[k, :, :bands] = folded[: 2 * hp]
+                    h_ref[k, :, fl : fl + bands] = folded[2 * hp :]
                 return carry
 
-            lax.fori_loop(0, count, prepare, 0)
-
+            lax.fori_loop(0, count // group, prepare, 0)
+
+        parts = stream(jnp.concatenate(transmit, axis=0), own_ref)
         arrive(2 * it)
         transmit = [t_ref[s] for s in range(slots)]
         befores, afters = neighbours(transmit, transmit, 2 * it)
-        domain = jnp.concatenate(
-            [
-                jnp.concatenate([befores[s], transmit[s], afters[s]], axis=1)
-                for s in range(slots)
-            ],
-            axis=0,
-        )
-        parts = stream(domain, spectrum_ref)
+        sides = [jnp.concatenate([befores[s], afters[s]], axis=1) for s in range(slots)]
+        parts = parts + stream(jnp.concatenate(sides, axis=0), side_ref)
         spectra = []
         for s in range(slots):
-            pr = parts[s * rows : (s + 1) * rows, :fl]
-            pi = parts[s * rows : (s + 1) * rows, fl:]
-            top = jnp.concatenate([pr, pi], axis=1)
-            low = jnp.concatenate([pi, -pr], axis=1)
-            spectra.append(table_dot(freqs_ref, jnp.concatenate([top, low], axis=0)) * unit)
+            folded = table_dot(freqs_ref, parts[s * rows : (s + 1) * rows]) * unit
+            ar, ai, br, bi = quarters(folded, hp, fl)
+            spectra.append((ar + bi, ai - br, ar - bi, ai + br))
 
         def forward(c, intensities):
             out = []
             for s in range(slots):
-                cr, ci = spectra[s][:, :fl], spectra[s][:, fl:]
+                pr, pi, mr, mi = spectra[s]
                 mids = []
                 for j in range(chunk):
                     k = c * chunk + j
-                    hr, hi = h_ref[k, :, :fl], h_ref[k, :, fl:]
-                    dr = hr * cr - hi * ci
-                    di = hr * ci + hi * cr
-                    top = jnp.concatenate([dr, di], axis=1)
-                    low = jnp.concatenate([-di, dr], axis=1)
-                    mids.append(table_dot(rows_ref, jnp.concatenate([top, low], axis=0)))
+                    hpr, hpi, hmr, hmi = quarters(h_ref[k], hp, fl)
+                    upr = hpr * pr - hpi * pi
+                    upi = hpr * pi + hpi * pr
+                    dnr = hmr * mr - hmi * mi
+                    dni = hmr * mi + hmi * mr
+                    mids.append(
+                        table_dot(rows_ref, block(upr + dnr, upi + dni, dni - upi, upr - dnr))
+                    )
                 fields = stream(jnp.concatenate(mids, axis=0), field_ref)
                 e_ref[s, c] = fields
                 total = intensities[s]
@@ -287,37 +342,38 @@
                     [fields[j * rows : (j + 1) * rows] * slopes[s] for j in range(chunk)], axis=0
                 )
                 columns = stream(back, adjoint_ref)
-                sr, si = sums[s]
+                spr, spi, smr, smi = sums[s]
                 for j in range(chunk):
                     k = c * chunk + j
-                    gr = columns[j * rows : (j + 1) * rows, :fl]
-                    gi = columns[j * rows : (j + 1) * rows, fl:]
-                    top = jnp.concatenate([gr, gi], axis=1)
-                    low = jnp.concatenate([-gi, gr], axis=1)
-                    freq = table_dot(freqs_ref, jnp.concatenate([top, low], axis=0))
-                    fr, fi = freq[:, :fl], freq[:, fl:]
-                    hr, hi = h_ref[k, :, :fl], h_ref[k, :, fl:]
-                    sr = sr + hr * fr - hi * fi
-                    si = si + hr * fi + hi * fr
-                out.append((sr, si))
+                    freq = table_dot(freqs_ref, columns[j * rows : (j + 1) * rows])
+                    ar, ai, br, bi = quarters(freq, hp, fl)
+                    hpr, hpi, hmr, hmi = quarters(h_ref[k], hp, fl)
+                    gpr, gpi, gmr, gmi = ar - bi, ai + br, ar + bi, ai - br
+                    spr = spr + hpr * gpr - hpi * gpi
+                    spi = spi + hpr * gpi + hpi * gpr
+                    smr = smr + hmr * gmr - hmi * gmi
+                    smi = smi + hmr * gmi + hmi * gmr
+                out.append((spr, spi, smr, smi))
             return tuple(out)
 
-        none = jnp.zeros((fp, fl), F32)
-        sums = lax.fori_loop(0, count // chunk, backward, ((none, none),) * slots)
+        none = jnp.zeros((hp, fl), F32)
+        sums = lax.fori_loop(0, count // chunk, backward, ((none,) * 4,) * slots)
 
         uppers = []
         for s in range(slots):
-            sr, si = sums[s]
-            top = jnp.concatenate([sr, si], axis=1)
-            low = jnp.concatenate([si, -sr], axis=1)
-            uppers.append(table_dot(rows_ref, jnp.concatenate([top, low], axis=0)))
-        grads = stream(jnp.concatenate(uppers, axis=0), gradient_ref) * (2.0 * unit)
-        to_left = [grads[s * rows : (s + 1) * rows, :cols] for s in range(slots)]
-        middle = [grads[s * rows : (s + 1) * rows, cols : 2 * cols] for s in range(slots)]
-        to_right = [grads[s * rows : (s + 1) * rows, 2 * cols :] for s in range(slots)]
+            spr, spi, smr, smi = sums[s]
+            uppers.append(
+                table_dot(rows_ref, block(spr + smr, spi + smi, spi - smi, smr - spr))
+            )
+        upper = jnp.concatenate(uppers, axis=0)
+        outer = stream(upper, outer_ref) * (2.0 * unit)
+        to_left = [outer[s * rows : (s + 1) * rows, :cols] for s in range(slots)]
+        to_right = [outer[s * rows : (s + 1) * rows, cols:] for s in range(slots)]
         send_ref[2 * it + 1, 0] = last_live(to_right)
         send_ref[2 * it + 1, 1] = to_left[0]
         start(2 * it + 1)
+        inner = stream(upper, middle_ref) * (2.0 * unit)
+        middle = [inner[s * rows : (s + 1) * rows] for s in range(slots)]
         arrive(2 * it + 1)
         befores, afters = neighbours(to_right, to_left, 2 * it + 1)
         for s in range(slots):
@@ -341,8 +397,9 @@
 def local(n, mask_params, target, weight, kernels, kernel_weight, tile_ids, tile_links):
     slots, rows, cols = mask_params.shape
     count, _, bands, _ = kernels.shape
-    fp, fl = round_up(bands, 16), round_up(bands, 128)
-    chunk = next(c for c in (4, 3, 2, 1) if count % c == 0)
+    hp, fl = round_up((bands - 1) // 2 + 1, 8), round_up(bands, 128)
+    chunk = next(c for c in (8, 4, 3, 2, 1) if count % c == 0)
+    flat = kernels.transpose(0, 2, 1, 3).reshape(count * bands * 2, bands)
     tables = make_tables(rows, cols, bands)
     vmem = pl.BlockSpec(memory_space=pltpu.VMEM)
     smem = pl.BlockSpec(memory_space=pltpu.SMEM)
@@ -350,16 +407,18 @@
     return pl.pallas_call(
         functools.partial(kernel, "tile", n, chunk),
         out_shape=(shape, shape),
-        in_specs=[vmem] * 4 + [smem] * 3 + [vmem] * len(tables),
+        in_specs=[vmem] * 3 + [pl.BlockSpec(memory_space=pl.ANY)] + [smem] * 3 + [vmem] * len(tables),
         out_specs=(vmem, vmem),
         scratch_shapes=[
-            pltpu.VMEM((count, fp, 2 * fl), F32),
+            pltpu.VMEM(flat.shape, F32),
+            pltpu.VMEM((count, 2 * hp, 2 * fl), F32),
             pltpu.VMEM((slots, count // chunk, chunk * rows, 2 * cols), F32),
             pltpu.VMEM((slots, rows, cols), F32),
             pltpu.VMEM((2 * ITERS, 2, rows, cols), F32),
             pltpu.VMEM((2 * ITERS, 2, rows, cols), F32),
             pltpu.SemaphoreType.DMA((2 * ITERS, 2)),
             pltpu.SemaphoreType.DMA((2 * ITERS, 2)),
+            pltpu.SemaphoreType.DMA,
         ],
         compiler_params=pltpu.CompilerParams(
             collective_id=0, has_side_effects=True, vmem_limit_bytes=48 * 1024 * 1024
@@ -368,7 +427,7 @@
         mask_params,
         target,
         weight,
-        kernels,
+        flat,
         kernel_weight,
         tile_ids,
         tile_links,

time: 43 us -> 47.7 us (1.11); the launches traced: 42.9 us -> 47 us
  local copies, waits for them, and re-layouts: 3.15 us -> 15.5 us
  Pallas kernels: 38.9 us -> 30.8 us
    unnamed x27 -> x34, local copies, waits for them, and re-layouts: 3.15 us -> 15.5 us
    pallas_call x1, Pallas kernels: 38.9 us -> 30.8 us  [local(): pl.pallas_call(functools.partial(kernel, 'tile', n, chunk), out_shape=(sh...]
where the time goes in v1:
time: 47.7 us; the launch traced here: 47 us
  Pallas kernels  30.8 us (65%)
  local copies, waits for them, and re-layouts  15.5 us (32%)
  between operations  0.66 us (1%)
    pallas_call x1, Pallas kernels, local(): pl.pallas_call(functools.partial(kernel, 'tile', n, chunk), out_shape=(sh...  30.8 us
    unnamed x34, local copies, waits for them, and re-layouts  15.5 us

profile of v1, /device:TPU:21, one launch (start us, length us, event | category | flops | bytes accessed | tf_op | source)
XLA Modules:
  0.0 47.0 jit_solution(2898316788648510593)
XLA Ops:
  0.6 0.0 copy-start
  0.6 1.4 %copy-done = f32[24,2,65,65]{3,1,2,0:T(2,128)S(1)} copy-done((f32[24,2,65,65]{3,1,2,0:T(2,128)S(1)}, f32[24,2,65,65]{3,1,2,0:T(2,128)}, u32[]{:S(2)}) %copy-start) | copy-done | bytes 811224
  2.0 0.0 copy-start.1
  2.1 1.0 %copy-done.1 = bf16[768,256]{1,0:T(8,128)(2,1)S(1)} copy-done((bf16[768,256]{1,0:T(8,128)(2,1)S(1)}, bf16[768,256]{1,0:T(8,128)(2,1)}, u32[]{:S(2)}) %copy-start.1) | copy-done | bytes 393240
  3.0 0.0 copy-start.2
  3.0 1.0 %copy-done.2 = bf16[768,256]{1,0:T(8,128)(2,1)S(1)} copy-done((bf16[768,256]{1,0:T(8,128)(2,1)S(1)}, bf16[768,256]{1,0:T(8,128)(2,1)}, u32[]{:S(2)}) %copy-start.2) | copy-done | bytes 393240
  4.0 0.0 copy-start.3
  4.0 1.0 %copy-done.3 = bf16[768,256]{1,0:T(8,128)(2,1)S(1)} copy-done((bf16[768,256]{1,0:T(8,128)(2,1)S(1)}, bf16[768,256]{1,0:T(8,128)(2,1)}, u32[]{:S(2)}) %copy-start.3) | copy-done | bytes 393240
  5.0 0.0 copy-start.4
  5.0 1.0 %copy-done.4 = bf16[768,256]{1,0:T(8,128)(2,1)S(1)} copy-done((bf16[768,256]{1,0:T(8,128)(2,1)S(1)}, bf16[768,256]{1,0:T(8,128)(2,1)}, u32[]{:S(2)}) %copy-start.4) | copy-done | bytes 393240
  6.0 0.0 copy-start.5
  6.0 1.0 %copy-done.5 = bf16[4,160,144]{2,1,0:T(8,128)(2,1)S(1)} copy-done((bf16[4,160,144]{2,1,0:T(8,128)(2,1)S(1)}, bf16[4,160,144]{2,1,0:T(8,128)(2,1)}, u32[]{:S(2)}) %copy-start.5) | copy-done | bytes 184344
  7.0 0.0 copy-start.6
  7.0 0.9 %copy-done.6 = bf16[768,128]{1,0:T(8,128)(2,1)S(1)} copy-done((bf16[768,128]{1,0:T(8,128)(2,1)S(1)}, bf16[768,128]{1,0:T(8,128)(2,1)}, u32[]{:S(2)}) %copy-start.6) | copy-done | bytes 196632
  7.9 0.9 %copy-done.7 = bf16[384,256]{1,0:T(8,128)(2,1)S(1)} copy-done((bf16[384,256]{1,0:T(8,128)(2,1)S(1)}, bf16[384,256]{1,0:T(8,128)(2,1)}, u32[]{:S(2)}) %copy-start.7) | copy-done | bytes 196632
  8.9 0.0 copy-start.8
  8.9 0.8 %copy-done.8 = f32[2,64,128]{2,1,0:T(8,128)S(1)} copy-done((f32[2,64,128]{2,1,0:T(8,128)S(1)}, f32[2,64,128]{2,1,0:T(8,128)}, u32[]{:S(2)}) %copy-start.8) | copy-done | bytes 65560
  9.7 0.0 copy-start.9
  9.7 0.8 %copy-done.9 = f32[2,64,128]{2,1,0:T(8,128)S(1)} copy-done((f32[2,64,128]{2,1,0:T(8,128)S(1)}, f32[2,64,128]{2,1,0:T(8,128)}, u32[]{:S(2)}) %copy-start.9) | copy-done | bytes 65560
  10.5 0.0 copy-start.10
  10.5 0.8 %copy-done.10 = f32[2,64,128]{2,1,0:T(8,128)S(1)} copy-done((f32[2,64,128]{2,1,0:T(8,128)S(1)}, f32[2,64,128]{2,1,0:T(8,128)}, u32[]{:S(2)}) %copy-start.10) | copy-done | bytes 65560
  11.4 0.0 copy-start.11
  11.4 0.8 %copy-done.11 = bf16[80,192]{1,0:T(8,128)(2,1)S(1)} copy-done((bf16[80,192]{1,0:T(8,128)(2,1)S(1)}, bf16[80,192]{1,0:T(8,128)(2,1)}, u32[]{:S(2)}) %copy-start.11) | copy-done | bytes 30744
  12.2 0.0 copy-start.12
  12.2 0.8 %copy-done.12 = bf16[64,240]{1,0:T(8,128)(2,1)S(1)} copy-done((bf16[64,240]{1,0:T(8,128)(2,1)S(1)}, bf16[64,240]{1,0:T(8,128)(2,1)}, u32[]{:S(2)}) %copy-start.12) | copy-done | bytes 30744
  12.9 0.0 copy-start.13
  12.9 0.7 %copy-done.13 = s32[2,2]{1,0:T(2,128)S(1)} copy-done((s32[2,2]{1,0:T(2,128)S(1)}, s32[2,2]{1,0:T(2,128)}, u32[]{:S(2)}) %copy-start.13) | copy-done | bytes 40
  13.6 0.7 %copy-done.14 = f32[24]{0:T(128)S(1)} copy-done((f32[24]{0:T(128)S(1)}, f32[24]{0:T(128)}, u32[]{:S(2)}) %copy-start.14) | copy-done | bytes 120
  14.3 0.7 %copy-done.15 = s32[2]{0:T(128)S(1)} copy-done((s32[2]{0:T(128)S(1)}, s32[2]{0:T(128)}, u32[]{:S(2)}) %copy-start.15) | copy-done | bytes 32
  14.9 30.8 %shard_map.167 = (f32[2,64,128]{2,1,0:T(8,128)S(1)}, f32[2,64,128]{2,1,0:T(8,128)S(1)}) custom-call(f32[2,64,128]{2,1,0:T(8,128)S(1)} %copy-done.8, f32[2,64,128]{2,1,0:T(8,128)S(1)} %copy-done.9, f32[2,64,128]{2,1,0:T(8,128)S(1)} %copy-done.10, f32[3120,65]{1,0:T(8,128)S(1)} %bitcast.3, f32[24]{0:T(128)S(1)} %copy-done.14, s32[2]{0:T(128)S(1)} %copy-done.15, ...), custom_call_target="tpu_custom_call" | custom-call | tf_op jit(solution)/shard_map/pallas_call | solution.py:407
  45.7 0.6 %copy.20 = f32[2,64,128]{2,1,0:T(8,128)} copy(f32[2,64,128]{2,1,0:T(8,128)S(1)} %get-tuple-element.4) | data formatting | bytes 131072
  46.3 0.6 %copy.21 = f32[2,64,128]{2,1,0:T(8,128)} copy(f32[2,64,128]{2,1,0:T(8,128)S(1)} %get-tuple-element.5) | data formatting | bytes 131072
  (3 shorter events, 0.0 us)
Async XLA Ops:
  0.6 1.4 %copy-start = (f32[24,2,65,65]{3,1,2,0:T(2,128)S(1)}, f32[24,2,65,65]{3,1,2,0:T(2,128)}, u32[]{:S(2)}) copy-start(f32[24,2,65,65]{3,1,2,0:T(2,128)} %param.19) | copy-start | bytes 2433604
  2.0 1.0 %copy-start.1 = (bf16[768,256]{1,0:T(8,128)(2,1)S(1)}, bf16[768,256]{1,0:T(8,128)(2,1)}, u32[]{:S(2)}) copy-start(bf16[768,256]{1,0:T(8,128)(2,1)} %constant.25.clone.outer_ref) | copy-start | bytes 1179652
  3.0 1.0 %copy-start.2 = (bf16[768,256]{1,0:T(8,128)(2,1)S(1)}, bf16[768,256]{1,0:T(8,128)(2,1)}, u32[]{:S(2)}) copy-start(bf16[768,256]{1,0:T(8,128)(2,1)} %constant.23.clone.adjoint_ref) | copy-start | bytes 1179652
  4.0 1.0 %copy-start.3 = (bf16[768,256]{1,0:T(8,128)(2,1)S(1)}, bf16[768,256]{1,0:T(8,128)(2,1)}, u32[]{:S(2)}) copy-start(bf16[768,256]{1,0:T(8,128)(2,1)} %constant.22.clone.field_ref) | copy-start | bytes 1179652
  5.0 1.0 %copy-start.4 = (bf16[768,256]{1,0:T(8,128)(2,1)S(1)}, bf16[768,256]{1,0:T(8,128)(2,1)}, u32[]{:S(2)}) copy-start(bf16[768,256]{1,0:T(8,128)(2,1)} %constant.21.clone.side_ref) | copy-start | bytes 1179652
  6.0 1.0 %copy-start.5 = (bf16[4,160,144]{2,1,0:T(8,128)(2,1)S(1)}, bf16[4,160,144]{2,1,0:T(8,128)(2,1)}, u32[]{:S(2)}) copy-start(bf16[4,160,144]{2,1,0:T(8,128)(2,1)} %constant.26.clone.fold_ref) | copy-start | bytes 552964
  7.0 0.9 %copy-start.6 = (bf16[768,128]{1,0:T(8,128)(2,1)S(1)}, bf16[768,128]{1,0:T(8,128)(2,1)}, u32[]{:S(2)}) copy-start(bf16[768,128]{1,0:T(8,128)(2,1)} %constant.24.clone.middle_ref) | copy-start | bytes 589828
  7.9 0.9 %copy-start.7 = (bf16[384,256]{1,0:T(8,128)(2,1)S(1)}, bf16[384,256]{1,0:T(8,128)(2,1)}, u32[]{:S(2)}) copy-start(bf16[384,256]{1,0:T(8,128)(2,1)} %constant.20.clone.own_ref) | copy-start | bytes 589828
  8.9 0.8 %copy-start.8 = (f32[2,64,128]{2,1,0:T(8,128)S(1)}, f32[2,64,128]{2,1,0:T(8,128)}, u32[]{:S(2)}) copy-start(f32[2,64,128]{2,1,0:T(8,128)} %params_ref.1) | copy-start | bytes 196612
  9.7 0.8 %copy-start.9 = (f32[2,64,128]{2,1,0:T(8,128)S(1)}, f32[2,64,128]{2,1,0:T(8,128)}, u32[]{:S(2)}) copy-start(f32[2,64,128]{2,1,0:T(8,128)} %target_ref.1) | copy-start | bytes 196612
  10.5 0.8 %copy-start.10 = (f32[2,64,128]{2,1,0:T(8,128)S(1)}, f32[2,64,128]{2,1,0:T(8,128)}, u32[]{:S(2)}) copy-start(f32[2,64,128]{2,1,0:T(8,128)} %weight_ref.1) | copy-start | bytes 196612
  11.4 0.8 %copy-start.11 = (bf16[80,192]{1,0:T(8,128)(2,1)S(1)}, bf16[80,192]{1,0:T(8,128)(2,1)}, u32[]{:S(2)}) copy-start(bf16[80,192]{1,0:T(8,128)(2,1)} %constant.19.clone.freqs_ref) | copy-start | bytes 92164
  12.2 0.8 %copy-start.12 = (bf16[64,240]{1,0:T(8,128)(2,1)S(1)}, bf16[64,240]{1,0:T(8,128)(2,1)}, u32[]{:S(2)}) copy-start(bf16[64,240]{1,0:T(8,128)(2,1)} %constant.18.clone.rows_ref) | copy-start | bytes 92164
  12.9 0.7 %copy-start.13 = (s32[2,2]{1,0:T(2,128)S(1)}, s32[2,2]{1,0:T(2,128)}, u32[]{:S(2)}) copy-start(s32[2,2]{1,0:T(2,128)} %links_ref.1) | copy-start | bytes 52
  13.6 0.7 %copy-start.14 = (f32[24]{0:T(128)S(1)}, f32[24]{0:T(128)}, u32[]{:S(2)}) copy-start(f32[24]{0:T(128)} %scale_ref.1) | copy-start | bytes 292
  14.3 0.7 %copy-start.15 = (s32[2]{0:T(128)S(1)}, s32[2]{0:T(128)}, u32[]{:S(2)}) copy-start(s32[2]{0:T(128)} %ids_ref.1) | copy-start | bytes 28

commit v2 on v1

--- a/solution.py
+++ b/solution.py
@@ -142,7 +142,7 @@
     params_ref,
     target_ref,
     weight_ref,
-    kernels_ref,
+    k_ref,
     scale_ref,
     ids_ref,
     links_ref,
@@ -157,7 +157,6 @@
     fold_ref,
     out_ref,
     resist_ref,
-    k_ref,
     h_ref,
     e_ref,
     t_ref,
@@ -165,7 +164,6 @@
     recv_ref,
     send_sems,
     recv_sems,
-    load_sem,
 ):
     me = lax.axis_index(axis)
     slots, rows, cols = params_ref.shape
@@ -176,8 +174,6 @@
     step_size = STEP_SCALE * math.sqrt(rows * cols)
     has_left, has_right = me > 0, me < n - 1
 
-    load = pltpu.make_async_copy(kernels_ref, k_ref, load_sem)
-    load.start()
     barrier = pltpu.get_barrier_semaphore()
 
     @pl.when(has_left)
@@ -264,8 +260,6 @@
         start(2 * it)
 
         if it == 0:
-
-            load.wait()
 
             def prepare(c, carry):
                 span = group * 2 * bands
@@ -394,23 +388,42 @@
             move(e, 1).wait_send()
 
 
+def staged(axis, n, chunk, held, inputs, *refs):
+    fixed, rest = list(refs[:inputs]), refs[inputs:]
+    buffers, sems = rest[-1 - len(held) : -1], rest[-1]
+    loads = [
+        pltpu.make_async_copy(fixed[i], buffer, sems.at[j])
+        for j, (i, buffer) in enumerate(zip(held, buffers))
+    ]
+    for load in loads:
+        load.start()
+    for load in loads:
+        load.wait()
+    for i, buffer in zip(held, buffers):
+        fixed[i] = buffer
+    kernel(axis, n, chunk, *fixed, *rest[: -1 - len(held)])
+
+
 def local(n, mask_params, target, weight, kernels, kernel_weight, tile_ids, tile_links):
     slots, rows, cols = mask_params.shape
     count, _, bands, _ = kernels.shape
     hp, fl = round_up((bands - 1) // 2 + 1, 8), round_up(bands, 128)
-    chunk = next(c for c in (8, 4, 3, 2, 1) if count % c == 0)
+    chunk = next(c for c in (12, 8, 4, 3, 2, 1) if count % c == 0)
     flat = kernels.transpose(0, 2, 1, 3).reshape(count * bands * 2, bands)
     tables = make_tables(rows, cols, bands)
     vmem = pl.BlockSpec(memory_space=pltpu.VMEM)
     smem = pl.BlockSpec(memory_space=pltpu.SMEM)
     shape = jax.ShapeDtypeStruct((slots, rows, cols), F32)
+    anywhere = pl.BlockSpec(memory_space=pl.ANY)
+    operands = [mask_params, target, weight, flat, kernel_weight, tile_ids, tile_links]
+    operands += [jnp.asarray(t) for t in tables]
+    held = [i for i in range(len(operands)) if i not in (4, 5, 6)]
     return pl.pallas_call(
-        functools.partial(kernel, "tile", n, chunk),
+        functools.partial(staged, "tile", n, chunk, held, len(operands)),
         out_shape=(shape, shape),
-        in_specs=[vmem] * 3 + [pl.BlockSpec(memory_space=pl.ANY)] + [smem] * 3 + [vmem] * len(tables),
+        in_specs=[anywhere] * 4 + [smem] * 3 + [anywhere] * len(tables),
         out_specs=(vmem, vmem),
         scratch_shapes=[
-            pltpu.VMEM(flat.shape, F32),
             pltpu.VMEM((count, 2 * hp, 2 * fl), F32),
             pltpu.VMEM((slots, count // chunk, chunk * rows, 2 * cols), F32),
             pltpu.VMEM((slots, rows, cols), F32),
@@ -418,21 +431,13 @@
             pltpu.VMEM((2 * ITERS, 2, rows, cols), F32),
             pltpu.SemaphoreType.DMA((2 * ITERS, 2)),
             pltpu.SemaphoreType.DMA((2 * ITERS, 2)),
-            pltpu.SemaphoreType.DMA,
+            *[pltpu.VMEM(operands[i].shape, operands[i].dtype) for i in held],
+            pltpu.SemaphoreType.DMA((len(held),)),
         ],
         compiler_params=pltpu.CompilerParams(
-            collective_id=0, has_side_effects=True, vmem_limit_bytes=48 * 1024 * 1024
+            collective_id=0, has_side_effects=True, vmem_limit_bytes=63 * 1024 * 1024
         ),
-    )(
-        mask_params,
-        target,
-        weight,
-        flat,
-        kernel_weight,
-        tile_ids,
-        tile_links,
-        *[jnp.asarray(t) for t in tables],
-    )
+    )(*operands)
 
 
 def solution(mesh):

time: 47.7 us -> 36.1 us (0.76)
  local copies, waits for them, and re-layouts: 15.5 us -> 2.95 us
  Pallas kernels: 30.8 us -> 32.2 us
    unnamed x34 -> x2, local copies, waits for them, and re-layouts: 15.5 us -> 2.95 us
    pallas_call x1, Pallas kernels: 30.8 us -> 32.2 us  [local(): pl.pallas_call(functools.partial(staged, 'tile', n, chunk, held, len(oper...]
where the time goes in v2:
time: 36.1 us; the launch traced here: 35.8 us
  Pallas kernels  32.2 us (89%)
  local copies, waits for them, and re-layouts  2.95 us (8%)
  between operations  0.64 us (2%)
    pallas_call x1, Pallas kernels, local(): pl.pallas_call(functools.partial(staged, 'tile', n, chunk, held, len(oper...  32.2 us
    unnamed x2, local copies, waits for them, and re-layouts  2.95 us

profile of v2, /device:TPU:21, one launch (start us, length us, event | category | flops | bytes accessed | tf_op | source)
XLA Modules:
  0.0 35.8 jit_solution(10485937251396782578)
XLA Ops:
  0.6 32.2 %shard_map.167 = (f32[2,64,128]{2,1,0:T(8,128)}, f32[2,64,128]{2,1,0:T(8,128)}) custom-call(f32[2,64,128]{2,1,0:T(8,128)} %refs_0_.1, f32[2,64,128]{2,1,0:T(8,128)} %refs_1_.1, f32[2,64,128]{2,1,0:T(8,128)} %refs_2_.1, f32[3120,65]{1,0:T(8,128)} %bitcast.3, f32[24]{0:T(128)} %refs_4_.1, s32[2]{0:T(128)} %refs_5_.1, s32[2,2]{1,0:T(2,128)} %refs_6_.1, ...), custom_call_target="tpu_custom_call" | custom-call | tf_op jit(solution)/shard_map/pallas_call | solution.py:421
  32.9 1.5 %copy.20 = f32[2,64,128]{2,1,0:T(8,128)} copy(f32[2,64,128]{2,1,0:T(8,128)} %get-tuple-element.4) | data formatting | bytes 131072
  34.4 1.5 %copy.21 = f32[2,64,128]{2,1,0:T(8,128)} copy(f32[2,64,128]{2,1,0:T(8,128)} %get-tuple-element.5) | data formatting | bytes 131072
